TPU v7x, 32 devices: a whole 2x2x4 slice. The times are simulated.
32 devices in a mesh: clip: 16 (over z, x, core), tm: 2 (over y).
Axes of the slice: x: 2, y: 2, z: 4, core: 2. Of those that a mesh axis runs over, the one named last changes fastest.
Arguments:
- clip_in: bfloat16 [16, 4, 8, 32, 128], P('clip', 'tm'), may hold values from -6 to 6
- cotangent: bfloat16 [16, 4, 8, 32, 128], P('clip', 'tm'), may hold values from -6 to 6
- spatial_w: bfloat16 [3, 3, 128, 128], replicated, may hold values from -0.1875 to 0.1875
- spatial_b: float32 [128], replicated, may hold values from -3 to 3
- temporal_w: bfloat16 [3, 128, 128], replicated, may hold values from -0.3125 to 0.3125
Outputs:
- grad_input: bfloat16 [16, 4, 8, 32, 128], P('clip', 'tm')
- grad_spatial_w: float32 [3, 3, 128, 128], replicated
- grad_spatial_b: float32 [128], replicated
- grad_temporal_w: float32 [3, 128, 128], replicated
All inputs are finite; a program needn't handle non-finite values.
Results may differ from a plain program's by a relative error of at most 0.006.
Values may be sent and summed in bfloat16 or wider, within the bound.
A program may use at most 64 MiB of HBM per device.

v0:
```python
import jax
import jax.numpy as jnp
from jax import lax
from jax.sharding import PartitionSpec as P


def spatial_forward(frames, weights, bias):
    count, height, width, chan = frames.shape
    padded = jnp.pad(frames, ((0, 0), (1, 1), (1, 1), (0, 0)))
    total = jnp.zeros((count * height * width, chan), jnp.float32)
    for i in range(3):
        for j in range(3):
            window = padded[:, i : i + height, j : j + width, :].reshape(-1, chan)
            total = total + jnp.dot(window, weights[i, j], preferred_element_type=jnp.float32)
    return (total + bias).reshape(count, height, width, chan)


def spatial_transpose(grads, weights):
    count, height, width, chan = grads.shape
    padded = jnp.pad(grads, ((0, 0), (1, 1), (1, 1), (0, 0)))
    total = jnp.zeros((count * height * width, chan), jnp.float32)
    for i in range(3):
        for j in range(3):
            window = padded[:, 2 - i : 2 - i + height, 2 - j : 2 - j + width, :].reshape(-1, chan)
            total = total + jnp.dot(window, weights[i, j].T, preferred_element_type=jnp.float32)
    return total.reshape(count, height, width, chan)


def spatial_weight_grad(frames, grads):
    count, height, width, chan = frames.shape
    padded = jnp.pad(frames, ((0, 0), (1, 1), (1, 1), (0, 0)))
    flat_grads = grads.reshape(-1, chan)
    result = []
    for i in range(3):
        row_terms = []
        for j in range(3):
            window = padded[:, i : i + height, j : j + width, :].reshape(-1, chan)
            row_terms.append(
                lax.dot_general(
                    window, flat_grads, (((0,), (0,)), ((), ())), preferred_element_type=jnp.float32
                )
            )
        result.append(jnp.stack(row_terms))
    return jnp.stack(result)


def temporal_back(act_before, act, cot, cot_after, temporal_w):
    count, height, width, chan = act.shape
    earlier = jnp.concatenate([act_before, act], axis=0)
    later = jnp.concatenate([cot, cot_after], axis=0)
    flat_cot = cot.reshape(-1, chan)
    grad_act = jnp.zeros((count * height * width, chan), jnp.float32)
    lag_terms = []
    for k in range(3):
        grad_act = grad_act + jnp.dot(
            later[k : k + count].reshape(-1, chan),
            temporal_w[k].T,
            preferred_element_type=jnp.float32,
        )
        shifted = earlier[2 - k : 2 - k + count].reshape(-1, chan)
        lag_terms.append(
            lax.dot_general(
                shifted, flat_cot, (((0,), (0,)), ((), ())), preferred_element_type=jnp.float32
            )
        )
    grad_act = grad_act.astype(jnp.bfloat16).reshape(count, height, width, chan)
    return (grad_act, jnp.stack(lag_terms))


def local(clip_in, cotangent, spatial_w, spatial_b, temporal_w):
    frames = clip_in[0]
    cot = cotangent[0]
    count, height, width, chan = frames.shape
    pre = spatial_forward(frames, spatial_w, spatial_b)
    act = jax.nn.silu(pre).astype(jnp.bfloat16)
    rows_act, rows_cot = (
        lax.all_to_all(act[None], "tm", split_axis=2, concat_axis=1, tiled=True),
        lax.all_to_all(cot[None], "tm", split_axis=2, concat_axis=1, tiled=True),
    )
    band_act = rows_act[0]
    band_cot = rows_cot[0]
    blank = jnp.zeros((2,) + band_act.shape[1:], jnp.bfloat16)
    band_grad, grad_tw = temporal_back(blank, band_act, band_cot, blank, temporal_w)
    grad_act = lax.all_to_all(band_grad[None], "tm", split_axis=1, concat_axis=2, tiled=True)[0]
    sig = jax.nn.sigmoid(pre)
    grad_pre = (grad_act.astype(jnp.float32) * sig * (1.0 + pre * (1.0 - sig))).astype(jnp.bfloat16)
    grad_in = (cot.astype(jnp.float32) + spatial_transpose(grad_pre, spatial_w)).astype(
        jnp.bfloat16
    )
    grad_sw = spatial_weight_grad(frames, grad_pre)
    grad_sb = jnp.sum(grad_pre.astype(jnp.float32).reshape(-1, chan), axis=0)
    grad_sw, grad_sb, grad_tw = lax.psum((grad_sw, grad_sb, grad_tw), "tm")
    grad_sw, grad_sb, grad_tw = lax.psum((grad_sw, grad_sb, grad_tw), "clip")
    total_cells = lax.axis_size("clip") * count * lax.axis_size("tm") * height * width
    norm = 1.0 / jnp.sqrt(jnp.float32(total_cells))
    return (grad_in[None], grad_sw * norm, grad_sb * norm, grad_tw * norm)


def solution(mesh):
    in_specs = (P("clip", "tm", None, None, None), P("clip", "tm", None, None, None), P(), P(), P())
    out_specs = (P("clip", "tm", None, None, None), P(), P(), P())
    return jax.shard_map(local, mesh=mesh, in_specs=in_specs, out_specs=out_specs, check_vma=False)
```

profile of v0, /device:TPU:0, one launch (start us, length us, event | category | flops | bytes accessed | tf_op | source)
XLA Modules:
  0.0 183.1 jit_solution(16784720149497251229)
XLA Ops:
  7.2 1.6 copy.15
  8.7 4.4 %all-to-all-start = ((bf16[1,2,8,32,128]{4,3,1,0,2:T(8,128)(2,1)}), bf16[1,2,8,32,128]{4,3,1,0,2:T(8,128)(2,1)S(1)}, u32[]{:S(2)}, u32[]{:S(2)}) async-start(bf16[1,2,8,32,128]{4,3,1,0,2:T(8,128)(2,1)} %copy.15), calls=%async_computation | async-start | bytes 262144 | tf_op jit(solution)/shard_map/all_to_all | solution.py:78
  13.3 0.8 copy-done.1
  15.3 2.4 %all-to-all-done = bf16[1,2,8,32,128]{4,3,1,0,2:T(8,128)(2,1)S(1)} async-done(((bf16[1,2,8,32,128]{4,3,1,0,2:T(8,128)(2,1)}), bf16[1,2,8,32,128]{4,3,1,0,2:T(8,128)(2,1)S(1)}, u32[]{:S(2)}, u32[]{:S(2)}) %all-to-all-start) | async-done | bytes 131104 | tf_op jit(solution)/shard_map/all_to_all | solution.py:78
  17.7 0.8 copy-done.4
  18.9 0.8 fusion.1
  19.8 3.4 %all-to-all-start.1 = ((bf16[1,4,4,32,128]{4,3,2,0,1:T(8,128)(2,1)}), bf16[1,4,4,32,128]{4,3,2,0,1:T(8,128)(2,1)S(1)}, u32[]{:S(2)}, u32[]{:S(2)}) async-start(bf16[1,4,4,32,128]{4,3,2,0,1:T(8,128)(2,1)} %bitcast.10), calls=%async_computation.1 | async-start | bytes 262144 | tf_op jit(solution)/shard_map/all_to_all | solution.py:84
  23.4 4.3 %all-to-all-done.1 = bf16[1,4,4,32,128]{4,3,2,0,1:T(8,128)(2,1)S(1)} async-done(((bf16[1,4,4,32,128]{4,3,2,0,1:T(8,128)(2,1)}), bf16[1,4,4,32,128]{4,3,2,0,1:T(8,128)(2,1)S(1)}, u32[]{:S(2)}, u32[]{:S(2)}) %all-to-all-start.1) | async-done | bytes 131104 | tf_op jit(solution)/shard_map/all_to_all | solution.py:84
  27.7 0.6 copy-done.5
  28.3 0.3 convert_reduce_fusion
  31.0 0.2 convolution_bitcast_fusion.7
  32.0 0.7 multiply_convert_fusion
  32.7 3.4 %all-to-all-start.2 = ((bf16[1,2,8,32,128]{4,3,1,0,2:T(8,128)(2,1)}), bf16[1,2,8,32,128]{4,3,1,0,2:T(8,128)(2,1)S(1)}, u32[]{:S(2)}, u32[]{:S(2)}) async-start(bf16[1,2,8,32,128]{4,3,1,0,2:T(8,128)(2,1)} %multiply_convert_fusion), calls=%async_computation.2 | async-start | bytes 262144 | tf_op jit(solution)/shard_map/all_to_all | solution.py:77
  36.2 0.9 pad_maximum_fusion
  37.0 3.5 %all-to-all-done.2 = bf16[1,2,8,32,128]{4,3,1,0,2:T(8,128)(2,1)S(1)} async-done(((bf16[1,2,8,32,128]{4,3,1,0,2:T(8,128)(2,1)}), bf16[1,2,8,32,128]{4,3,1,0,2:T(8,128)(2,1)S(1)}, u32[]{:S(2)}, u32[]{:S(2)}) %all-to-all-start.2) | async-done | bytes 131104 | tf_op jit(solution)/shard_map/all_to_all | solution.py:77
  41.3 0.7 pad_maximum_fusion.1
  42.2 4.9 %psum.44 = f32[128]{0:T(128)S(1)} all-reduce(f32[128]{0:T(128)S(1)} %get-tuple-element.8), channel_id=1, replica_groups=mesh['clip'=16,'tm'=2] {'tm'}, use_global_device_ids=true, to_apply=%region_3.4 | all-reduce | flops 128 | bytes 1024 | tf_op jit(solution)/shard_map/psum | solution.py:92
  47.2 29.7 %psum.45 = f32[128]{0:T(128)S(1)} all-reduce(f32[128]{0:T(128)S(1)} %psum.44), channel_id=1, replica_groups=mesh['clip'=16,'tm'=2] {'clip'}, use_global_device_ids=true, to_apply=%region_4.5 | all-reduce | flops 128 | bytes 1024 | tf_op jit(solution)/shard_map/psum | solution.py:93
  77.5 0.5 broadcast_multiply_fusion.2
  78.1 0.4 copy-done.2
  78.4 0.7 add_convert_fusion
  79.1 94.5 %all-reduce.9.cloned.1.call-done = (f32[3,3,128,128]{3,2,1,0:T(8,128)}, f32[3,128,128]{2,1,0:T(8,128)}) async-done(((f32[3,3,128,128]{3,2,1,0:T(8,128)}, f32[3,128,128]{2,1,0:T(8,128)}), (f32[3,3,128,128]{3,2,1,0:T(8,128)}, f32[3,128,128]{2,1,0:T(8,128)})) %all-reduce.9.cloned.1.call-update) | async-done | bytes 786448 | tf_op jit(solution)/shard_map/psum | solution.py:93
  173.6 2.0 %broadcast_multiply_fusion = f32[3,3,128,128]{3,2,1,0:T(8,128)} fusion(f32[3,3,128,128]{3,2,1,0:T(8,128)} %get-tuple-element.4), kind=kLoop, calls=%fused_computation.33 | loop fusion | flops 147456 | bytes 1179648 | tf_op jit(solution)/shard_map/mul | solution.py:96
  175.6 0.7 broadcast_multiply_fusion.1
  (53 shorter events, 6.6 us)
Async XLA Ops:
  8.7 4.4 %copy-start = (bf16[1,2,8,32,128]{4,3,2,1,0:T(8,128)(2,1)S(1)}, bf16[1,2,8,32,128]{4,3,2,1,0:T(8,128)(2,1)}, u32[]{:S(2)}) copy-start(bf16[1,2,8,32,128]{4,3,2,1,0:T(8,128)(2,1)} %param.5) | copy-start | bytes 393220
  8.7 8.9 %all-to-all-start = ((bf16[1,2,8,32,128]{4,3,1,0,2:T(8,128)(2,1)}), bf16[1,2,8,32,128]{4,3,1,0,2:T(8,128)(2,1)S(1)}, u32[]{:S(2)}, u32[]{:S(2)}) async-start(bf16[1,2,8,32,128]{4,3,1,0,2:T(8,128)(2,1)} %copy.15), calls=%async_computation | async-start | bytes 262144 | tf_op jit(solution)/shard_map/all_to_all | solution.py:78
  13.1 1.0 copy-start.1
  17.7 0.9 copy-start.4
  19.8 7.8 %all-to-all-start.1 = ((bf16[1,4,4,32,128]{4,3,2,0,1:T(8,128)(2,1)}), bf16[1,4,4,32,128]{4,3,2,0,1:T(8,128)(2,1)S(1)}, u32[]{:S(2)}, u32[]{:S(2)}) async-start(bf16[1,4,4,32,128]{4,3,2,0,1:T(8,128)(2,1)} %bitcast.10), calls=%async_computation.1 | async-start | bytes 262144 | tf_op jit(solution)/shard_map/all_to_all | solution.py:84
  27.7 0.7 copy-start.5
  32.7 7.8 %all-to-all-start.2 = ((bf16[1,2,8,32,128]{4,3,1,0,2:T(8,128)(2,1)}), bf16[1,2,8,32,128]{4,3,1,0,2:T(8,128)(2,1)S(1)}, u32[]{:S(2)}, u32[]{:S(2)}) async-start(bf16[1,2,8,32,128]{4,3,1,0,2:T(8,128)(2,1)} %multiply_convert_fusion), calls=%async_computation.2 | async-start | bytes 262144 | tf_op jit(solution)/shard_map/all_to_all | solution.py:77
  36.1 41.4 %all-reduce.11.cloned.1.call-start = ((), (), s32[]{:S(2)}) async-start(), calls=%async_computation.4 | async-start | bytes 1572864 | tf_op jit(solution)/shard_map/psum | solution.py:92
  42.0 131.6 %all-reduce.9.cloned.1.call-start = ((), (), s32[]{:S(2)}) async-start(), calls=%async_computation.3 | async-start | bytes 1572864 | tf_op jit(solution)/shard_map/psum | solution.py:93
  77.5 0.9 copy-start.2
  173.6 2.0 %copy-start.3 = (f32[3,128,128]{2,1,0:T(8,128)S(1)}, f32[3,128,128]{2,1,0:T(8,128)}, u32[]{:S(2)}) copy-start(f32[3,128,128]{2,1,0:T(8,128)} %get-tuple-element.5) | copy-start | bytes 589828
Sparse Core Ops, SparseCore 0:
  42.1 35.2 all-reduce.10
  81.3 92.2 all-reduce.8
where the time goes:
time: 184 us; the launch traced here: 183 us
  waiting for transfers between devices  105 us (57%)
  blocking collectives  34.7 us (19%)
  between operations  14.4 us (8%)
  starting transfers between devices  11.2 us (6%)
  matrix products  7.23 us (4%)
  other arithmetic  6.3 us (3%)
  local copies, waits for them, and re-layouts  4.65 us (3%)
    psum x1, waiting for transfers between devices, local(): grad_sw, grad_sb, grad_tw = lax.psum((grad_sw, grad_sb, grad_tw), 'clip')  94.5 us
    psum x1, blocking collectives, local(): grad_sw, grad_sb, grad_tw = lax.psum((grad_sw, grad_sb, grad_tw), 'clip')  29.7 us
    psum x1, blocking collectives, local(): grad_sw, grad_sb, grad_tw = lax.psum((grad_sw, grad_sb, grad_tw), 'tm')  4.94 us
    all_to_all x1, starting transfers between devices, local(): lax.all_to_all(cot[None], 'tm', split_axis=2, concat_axis=1, tiled=True)  4.37 us
    all_to_all x1, waiting for transfers between devices, local(): lax.all_to_all(band_grad[None], 'tm', split_axis=1, concat_axis=2, tiled=...  4.28 us
    unnamed x13, local copies, waits for them, and re-layouts  4.24 us
  transfers between devices with their start and end apart: 5, of which 4 were waited for; matrix products, arithmetic and copies ran while one was open for 2% of the time, Pallas kernels for 0%

commit v1 on v0

v1 whole, which is shorter than its diff:
```python
import functools

import jax
import jax.numpy as jnp
from jax import lax
from jax.experimental import pallas as pl
from jax.experimental.pallas import tpu as pltpu
from jax.sharding import PartitionSpec as P

MESH = pl.DeviceIdType.MESH
F32, BF16 = jnp.float32, jnp.bfloat16
TILE = 16
CHUNKS = 1


def bits_of(size):
    count = size.bit_length() - 1
    assert 1 << count == size
    return count


def make_plan(clips, tms, rows):
    clip_bits, tm_bits = bits_of(clips), bits_of(tms)
    groups = [
        [("clip", 0)][:clip_bits],
        [("tm", b) for b in range(tm_bits)] + [("clip", b) for b in range(1, clip_bits) if b < 2],
        [("clip", b) for b in range(2, clip_bits)],
    ]
    plan = []
    for order, group in enumerate(groups):
        kind = F32 if order == 0 else BF16
        cut = len(group)
        while rows % (TILE << cut):
            cut -= 1
        if cut:
            plan.append((tuple(group[:cut]), True, rows, rows >> cut, kind))
            rows >>= cut
        if cut < len(group):
            plan.append((tuple(group[cut:]), False, rows, rows, kind))
    return plan


def kernel(plan, chunk_rows, tms, *refs):
    x_ref, cot_ref, sw_ref, sb_ref, tw_ref, gin_ref, grads_ref, bias_ref = refs[:8]
    next_cot, pad3, acc, res, cot_send, cot_recv = refs[8:14]
    phases, position = [], 14
    for _ in plan:
        phases.append(refs[position : position + 12])
        position += 12
    frames, height, width, chan = x_ref.shape[1:]
    area = height * width
    pixels = frames * area
    chunks = acc.shape[0]
    me = {"clip": lax.axis_index("clip"), "tm": lax.axis_index("tm")}

    def bit(which):
        axis, b = which
        return lax.rem(me[axis] // (1 << b), 2)

    def group_index(group):
        return sum((bit(w) * (1 << n) for n, w in enumerate(group)), 0)

    def partner(group, m):
        to = dict(me)
        index = group_index(group)
        for n, which in enumerate(group):
            if (m >> n) & 1:
                axis, b = which
                to[axis] = to[axis] + (1 - 2 * bit(which)) * (1 << b)
                index = index + (1 - 2 * bit(which)) * (1 << n)
        return to, index

    barrier = pltpu.get_barrier_semaphore()
    greeted = 0
    for group, *_ in plan:
        for m in range(1, 1 << len(group)):
            pl.semaphore_signal(barrier, inc=1, device_id=partner(group, m)[0], device_id_type=MESH)
            greeted += 1
    pl.semaphore_wait(barrier, greeted)

    tm = me["tm"]
    cot_copy = pltpu.make_async_remote_copy(
        src_ref=cot_ref.at[0, pl.ds(0, 2)],
        dst_ref=next_cot,
        send_sem=cot_send,
        recv_sem=cot_recv,
        device_id={"clip": me["clip"], "tm": jnp.maximum(tm - 1, 0)},
        device_id_type=MESH,
    )

    @pl.when(tm > 0)
    def _():
        cot_copy.start()

    column = lax.broadcasted_iota(jnp.int32, (pixels, chan), 0) % width

    def column_shift(flat, d):
        if d == 0:
            return flat.astype(BF16)
        rolled = pltpu.roll(flat, (-d) % pixels, 0)
        edge = width - 1 if d == 1 else 0
        return jnp.where(column == edge, 0.0, rolled).astype(BF16)

    def fill(flat, sign):
        for j in range(3):
            moved = column_shift(flat, sign * (j - 1)).reshape(frames, area, chan)
            pad3[:, pl.ds(width, area), pl.ds(j * chan, chan)] = moved

    def window(start):
        return pad3[:, pl.ds(start * width, area), :].reshape(pixels, 3 * chan)

    blank = jnp.zeros((frames, width, 3 * chan), BF16)
    pad3[:, pl.ds(0, width), :] = blank
    pad3[:, pl.ds(width + area, width), :] = blank

    x = x_ref[0].reshape(pixels, chan)
    fill(x.astype(F32), 1)
    pre = jnp.zeros((pixels, chan), F32)
    for i in range(3):
        pre = pre + jnp.dot(
            window(i), sw_ref[i].reshape(3 * chan, chan), preferred_element_type=F32
        )
    pre = pre + sb_ref[...]
    sig = 1.0 / (1.0 + jnp.exp(-pre))
    act = (pre * sig).astype(BF16)
    slope = sig * (1.0 + pre * (1.0 - sig))
    act_t = act.astype(F32).T.astype(BF16)
    x_t = x.astype(F32).T.astype(BF16)

    last = tm == tms - 1

    @pl.when(last)
    def _():
        next_cot[...] = jnp.zeros_like(next_cot)

    @pl.when(jnp.logical_not(last))
    def _():
        cot_copy.wait_recv()

    cot = cot_ref[0].reshape(pixels, chan)
    after = next_cot[...].reshape(2 * area, chan)
    later = [cot]
    for k in (1, 2):
        kept = [cot[k * area :]] if k < frames else []
        later.append(jnp.concatenate(kept + [after[: k * area]], axis=0))
    later = jnp.concatenate(later, axis=1)
    nt = (((1,), (1,)), ((), ()))
    tw = jnp.concatenate([tw_ref[k] for k in range(3)], axis=1)
    grad_act = lax.dot_general(later, tw, nt, preferred_element_type=F32).astype(BF16)
    grad_pre = (grad_act.astype(F32) * slope).astype(BF16)
    grad_pre32 = grad_pre.astype(F32)
    fill(grad_pre32, -1)

    def put(block, value):
        row = block * chan
        c = row // chunk_rows
        acc[c, pl.ds(row - c * chunk_rows, chan), :] = value

    grad_tw = jnp.dot(act_t, later, preferred_element_type=F32)
    for k in range(3):
        put(k, grad_tw[:, k * chan : (k + 1) * chan])

    def spatial_row(i):
        grad = jnp.dot(x_t, window(2 - i), preferred_element_type=F32)
        for j in range(3):
            put(3 + 3 * i + j, grad[:, j * chan : (j + 1) * chan])

    def input_grad():
        total = cot.astype(F32)
        for i in range(3):
            sw = jnp.concatenate([sw_ref[i, j] for j in range(3)], axis=1)
            total = total + lax.dot_general(window(2 - i), sw, nt, preferred_element_type=F32)
        gin_ref[0] = total.astype(BF16).reshape(frames, height, width, chan)

    offsets = [0]
    for group, scatter, _, share, _ in plan:
        offsets.append(offsets[-1] + (group_index(group) * share if scatter else 0))
    pending = []

    def start(copy):
        copy.start()
        pending.append(copy)
        return copy

    waiting = {}

    def share_at(index, share):
        return pl.ds(pl.multiple_of(index * share, TILE), share)

    def reduce_start(c, p):
        group, scatter, rows, share, kind = plan[p]
        cur, stage, recv, bsend, brecv = phases[p][:5]
        ss, rs, bss, brs = phases[p][6:10]
        index = group_index(group)
        source = cur
        if p == 0:
            source = acc
        if kind != F32:
            stage[c] = source[c].astype(kind)
            outgoing = stage
        else:
            outgoing = source
        copies = []
        for m in range(1, 1 << len(group)):
            to, their = partner(group, m)
            src = outgoing.at[c, share_at(their, share)] if scatter else outgoing.at[c]
            copies.append(
                start(
                    pltpu.make_async_remote_copy(
                        src_ref=src,
                        dst_ref=recv.at[c, index],
                        send_sem=ss.at[c, m],
                        recv_sem=rs.at[c, m],
                        device_id=to,
                        device_id_type=MESH,
                    )
                )
            )
            if c == chunks - 1:
                copies.append(
                    start(
                        pltpu.make_async_remote_copy(
                            src_ref=bsend,
                            dst_ref=brecv.at[index],
                            send_sem=bss.at[m],
                            recv_sem=brs.at[m],
                            device_id=to,
                            device_id_type=MESH,
                        )
                    )
                )
        waiting[c] = copies

    def reduce_end(c, p):
        group, scatter, rows, share, kind = plan[p]
        cur, stage, recv, bsend, brecv = phases[p][:5]
        index = group_index(group)
        source = acc if p == 0 else cur
        own = source[c, share_at(index, share)] if scatter else source[c]
        recv[c, index] = own.astype(kind)
        if c == chunks - 1:
            brecv[index] = bsend[...]
        for copy in waiting[c]:
            copy.wait_recv()
        total = recv[c, 0].astype(F32)
        for n in range(1, 1 << len(group)):
            total = total + recv[c, n].astype(F32)
        if c == chunks - 1:
            bias = brecv[0]
            for n in range(1, 1 << len(group)):
                bias = bias + brecv[n]
            if p + 1 < len(plan):
                phases[p + 1][3][...] = bias
            else:
                bias_ref[...] = bias
        if p + 1 < len(plan):
            phases[p + 1][0][c] = total
        else:
            res[c, pl.ds(pl.multiple_of(offsets[-1], TILE), share)] = total.astype(BF16)

    def gather_start(c, p):
        group, scatter, rows, share, kind = plan[p]
        gs, gr = phases[p][10:12]
        copies = []
        mine = res.at[c, pl.ds(pl.multiple_of(offsets[p + 1], TILE), share)]
        for m in range(1, 1 << len(group)):
            to, _ = partner(group, m)
            copies.append(
                start(
                    pltpu.make_async_remote_copy(
                        src_ref=mine,
                        dst_ref=mine,
                        send_sem=gs.at[c, m],
                        recv_sem=gr.at[c, m],
                        device_id=to,
                        device_id_type=MESH,
                    )
                )
            )
        waiting[c] = copies

    def gather_end(c, p):
        for copy in waiting[c]:
            copy.wait_recv()

    steps = []
    for p in range(len(plan)):
        steps.append((reduce_start, reduce_end, p))
    for p in reversed(range(len(plan))):
        if plan[p][1]:
            steps.append((gather_start, gather_end, p))

    def advance(c, k):
        if k > 0:
            steps[k - 1][1](c, steps[k - 1][2])
        if k < len(steps):
            steps[k][0](c, steps[k][2])
        else:
            grads_ref[pl.ds(c * chunk_rows, chunk_rows)] = res[c]

    phases[0][3][...] = jnp.sum(grad_pre32.reshape(pixels // 8, 8, chan), axis=0)
    for i in range(3):
        spatial_row(i)
    for c in range(chunks):
        advance(c, 0)
    input_grad()
    for step in range(1, len(steps) + chunks):
        for c in range(chunks):
            if 1 <= step - c <= len(steps):
                advance(c, step - c)
    for copy in pending:
        copy.wait_send()

    @pl.when(tm > 0)
    def _():
        cot_copy.wait_send()


def local(clips, tms, clip_in, cotangent, spatial_w, spatial_b, temporal_w):
    _, frames, height, width, chan = clip_in.shape
    assert frames == 2
    total_rows = 12 * chan
    chunk_rows = total_rows // CHUNKS
    plan = make_plan(clips, tms, chunk_rows)
    scratch = [
        pltpu.VMEM((2, height, width, chan), BF16),
        pltpu.VMEM((frames, (height + 2) * width, 3 * chan), BF16),
        pltpu.VMEM((CHUNKS, chunk_rows, chan), F32),
        pltpu.VMEM((CHUNKS, chunk_rows, chan), BF16),
        pltpu.SemaphoreType.DMA,
        pltpu.SemaphoreType.DMA,
    ]
    for order, (group, scatter, rows, share, kind) in enumerate(plan):
        n = 1 << len(group)
        sems = pltpu.SemaphoreType.DMA((CHUNKS, n))
        scratch += [
            pltpu.VMEM((CHUNKS, rows, chan) if order else (1, 8, chan), F32),
            pltpu.VMEM((CHUNKS, rows, chan) if kind != F32 else (1, TILE, chan), BF16),
            pltpu.VMEM((CHUNKS, n, share, chan), kind),
            pltpu.VMEM((8, chan), F32),
            pltpu.VMEM((n, 8, chan), F32),
            pltpu.VMEM((8, chan), F32),
            sems,
            sems,
            pltpu.SemaphoreType.DMA((n,)),
            pltpu.SemaphoreType.DMA((n,)),
            sems,
            sems,
        ]
    vmem = pl.BlockSpec(memory_space=pltpu.VMEM)
    grad_in, grads, bias = pl.pallas_call(
        functools.partial(kernel, plan, chunk_rows, tms),
        out_shape=(
            jax.ShapeDtypeStruct(clip_in.shape, BF16),
            jax.ShapeDtypeStruct((total_rows, chan), BF16),
            jax.ShapeDtypeStruct((8, chan), F32),
        ),
        in_specs=[vmem] * 5,
        out_specs=(vmem, vmem, vmem),
        scratch_shapes=scratch,
        compiler_params=pltpu.CompilerParams(
            collective_id=0, has_side_effects=True, vmem_limit_bytes=48 * 1024 * 1024
        ),
        name="block_backward",
    )(clip_in, cotangent, spatial_w, spatial_b.reshape(1, chan), temporal_w)
    norm = 1.0 / jnp.sqrt(F32(clips * tms * frames * height * width))
    grads = grads.astype(F32) * norm
    return (
        grad_in,
        grads[3 * chan :].reshape(3, 3, chan, chan),
        jnp.sum(bias, axis=0) * norm,
        grads[: 3 * chan].reshape(3, chan, chan),
    )


def solution(mesh):
    block = P("clip", "tm", None, None, None)
    return jax.shard_map(
        functools.partial(local, mesh.shape["clip"], mesh.shape["tm"]),
        mesh=mesh,
        in_specs=(block, block, P(), P(), P()),
        out_specs=(block, P(), P(), P()),
        check_vma=False,
    )
```

time: 184 us -> 37.5 us (0.20)
  waiting for transfers between devices: 105 us -> 0 us
  blocking collectives: 34.7 us -> 0 us
  Pallas kernels: 0 us -> 29.6 us
  between operations: 14.4 us -> 0.66 us
  starting transfers between devices: 11.2 us -> 0 us
  matrix products: 7.23 us -> 0 us
  other arithmetic: 6.3 us -> 0.59 us
  local copies, waits for them, and re-layouts: 4.65 us -> 6.51 us
    psum x2 -> x0, waiting for transfers between devices: 94.5 us -> none  [the longest x1 94.5 us: local(): grad_sw, grad_sb, grad_tw = lax.psum((grad_sw, grad_sb, grad_tw), 'clip')]
    psum x2 -> x0, blocking collectives: 34.7 us -> none  [the longest x1 29.7 us: local(): grad_sw, grad_sb, grad_tw = lax.psum((grad_sw, grad_sb, grad_tw), 'clip')]
    pallas_call x0 -> x1, Pallas kernels: none -> 29.6 us  [local(): pl.pallas_call(functools.partial(kernel, plan, chunk_rows, tms), out_shap...]
    all_to_all x3 -> x0, starting transfers between devices: 11.1 us -> none  [the longest x1 4.37 us: local(): lax.all_to_all(cot[None], 'tm', split_axis=2, concat_axis=1, tiled=True)]
    all_to_all x3 -> x0, waiting for transfers between devices: 10.1 us -> none  [the longest x1 4.28 us: local(): lax.all_to_all(band_grad[None], 'tm', split_axis=1, concat_axis=2, tiled=...]
    dot_general x33 -> x0, matrix products: 7.23 us -> none  [the longest x9 2.04 us: spatial_weight_grad(): lax.dot_general(window, flat_grads, (((0,), (0,)), ((), ())), preferred_e...]
    mul x3 -> x2, other arithmetic: 3.16 us -> 0.57 us  [the longest x1 0.52 us: local(): jnp.sum(bias, axis=0) * norm]
    unnamed x13 -> x11, local copies, waits for them, and re-layouts: 4.24 us -> 4.96 us
  transfers between devices with their start and end apart: 5 -> 0, of which waited for: 4 -> 0; matrix products, arithmetic and copies ran while one was open for 2% -> 0% of each run, Pallas kernels for 0% -> 0%
where the time goes in v1:
time: 37.5 us; the launch traced here: 37.3 us
  Pallas kernels  29.6 us (79%)
  local copies, waits for them, and re-layouts  6.51 us (17%)
  between operations  0.66 us (2%)
  other arithmetic  0.59 us (2%)
    pallas_call x1, Pallas kernels, local(): pl.pallas_call(functools.partial(kernel, plan, chunk_rows, tms), out_shap...  29.6 us
    unnamed x11, local copies, waits for them, and re-layouts  4.96 us
    slice x1, local copies, waits for them, and re-layouts, local(): grads[3 * chan:].reshape(3, 3, chan, chan)  0.85 us

profile of v1, /device:TPU:0, one launch (start us, length us, event | category | flops | bytes accessed | tf_op | source)
XLA Modules:
  0.0 37.3 jit_solution(7465694267113501795)
XLA Ops:
  0.6 0.0 copy-start.4
  0.6 0.6 %copy-done.4 = f32[128]{0:T(128)S(1)} copy-done((f32[128]{0:T(128)S(1)}, f32[128]{0:T(128)}, u32[]{:S(2)}) %copy-start.4) | copy-done | bytes 536
  1.3 0.0 copy-start
  1.3 1.0 %copy-done = bf16[3,3,128,128]{3,2,1,0:T(8,128)(2,1)S(1)} copy-done((bf16[3,3,128,128]{3,2,1,0:T(8,128)(2,1)S(1)}, bf16[3,3,128,128]{3,2,1,0:T(8,128)(2,1)}, u32[]{:S(2)}) %copy-start) | copy-done | bytes 294936
  2.3 0.0 copy-start.1
  2.3 0.9 %copy-done.1 = bf16[1,2,8,32,128]{4,3,2,1,0:T(8,128)(2,1)S(1)} copy-done((bf16[1,2,8,32,128]{4,3,2,1,0:T(8,128)(2,1)S(1)}, bf16[1,2,8,32,128]{4,3,2,1,0:T(8,128)(2,1)}, u32[]{:S(2)}) %copy-start.1) | copy-done | bytes 131096
  3.2 0.0 copy-start.2
  3.2 0.9 %copy-done.2 = bf16[1,2,8,32,128]{4,3,2,1,0:T(8,128)(2,1)S(1)} copy-done((bf16[1,2,8,32,128]{4,3,2,1,0:T(8,128)(2,1)S(1)}, bf16[1,2,8,32,128]{4,3,2,1,0:T(8,128)(2,1)}, u32[]{:S(2)}) %copy-start.2) | copy-done | bytes 131096
  4.1 0.0 copy-start.3
  4.1 0.9 %copy-done.3 = bf16[3,128,128]{2,1,0:T(8,128)(2,1)S(1)} copy-done((bf16[3,128,128]{2,1,0:T(8,128)(2,1)S(1)}, bf16[3,128,128]{2,1,0:T(8,128)(2,1)}, u32[]{:S(2)}) %copy-start.3) | copy-done | bytes 98328
  5.0 29.6 %block_backward.1 = (bf16[1,2,8,32,128]{4,3,2,1,0:T(8,128)(2,1)S(1)}, bf16[1536,128]{1,0:T(8,128)(2,1)S(1)}, f32[8,128]{1,0:T(8,128)S(1)}) custom-call(bf16[1,2,8,32,128]{4,3,2,1,0:T(8,128)(2,1)S(1)} %copy-done.1, bf16[1,2,8,32,128]{4,3,2,1,0:T(8,128)(2,1)S(1)} %copy-done.2, bf16[3,3,128,128]{3,2,1,0:T(8,128)(2,1)S(1)} %copy-done, f32[1,128]{1,0:T(1,128)S(1)} %bitcast.3, ...), custom_call_target="tpu_custom_call" | custom-call | tf_op jit(solution)/shard_map/block_backward/pallas_call | solution.py:351
  34.5 0.5 %broadcast_multiply_fusion = f32[128]{0:T(128)} fusion(f32[128]{0:T(128)S(1)} %reduce_sum.9), kind=kLoop, calls=%fused_computation.1 | loop fusion | flops 128 | bytes 1024 | tf_op jit(solution)/shard_map/mul | solution.py:371
  35.0 0.1 convert_multiply_fusion
  35.1 0.7 %slice.9 = f32[384,128]{1,0:T(8,128)} slice(f32[1536,128]{1,0:T(8,128)S(1)} %convert_multiply_fusion), slice={[0:384], [0:128]} | slice | bytes 393216 | tf_op jit(solution)/shard_map/slice | solution.py:372
  35.8 0.9 %slice.8 = f32[1152,128]{1,0:T(8,128)} slice(f32[1536,128]{1,0:T(8,128)S(1)} %convert_multiply_fusion), slice={[384:1536], [0:128]} | slice | bytes 1179648 | tf_op jit(solution)/shard_map/slice | solution.py:370
  36.6 0.7 %copy.10 = bf16[1,2,8,32,128]{4,3,2,1,0:T(8,128)(2,1)} copy(bf16[1,2,8,32,128]{4,3,2,1,0:T(8,128)(2,1)S(1)} %get-tuple-element.14) | data formatting | bytes 262144
  (1 shorter events, 0.0 us)
Async XLA Ops:
  0.6 0.7 %copy-start.4 = (f32[128]{0:T(128)S(1)}, f32[128]{0:T(128)}, u32[]{:S(2)}) copy-start(f32[128]{0:T(128)} %param.8) | copy-start | bytes 1540
  1.3 1.0 %copy-start = (bf16[3,3,128,128]{3,2,1,0:T(8,128)(2,1)S(1)}, bf16[3,3,128,128]{3,2,1,0:T(8,128)(2,1)}, u32[]{:S(2)}) copy-start(bf16[3,3,128,128]{3,2,1,0:T(8,128)(2,1)} %refs_2_.1) | copy-start | bytes 884740
  2.3 0.9 %copy-start.1 = (bf16[1,2,8,32,128]{4,3,2,1,0:T(8,128)(2,1)S(1)}, bf16[1,2,8,32,128]{4,3,2,1,0:T(8,128)(2,1)}, u32[]{:S(2)}) copy-start(bf16[1,2,8,32,128]{4,3,2,1,0:T(8,128)(2,1)} %refs_0_.1) | copy-start | bytes 393220
  3.2 0.9 %copy-start.2 = (bf16[1,2,8,32,128]{4,3,2,1,0:T(8,128)(2,1)S(1)}, bf16[1,2,8,32,128]{4,3,2,1,0:T(8,128)(2,1)}, u32[]{:S(2)}) copy-start(bf16[1,2,8,32,128]{4,3,2,1,0:T(8,128)(2,1)} %refs_1_.1) | copy-start | bytes 393220
  4.1 0.9 %copy-start.3 = (bf16[3,128,128]{2,1,0:T(8,128)(2,1)S(1)}, bf16[3,128,128]{2,1,0:T(8,128)(2,1)}, u32[]{:S(2)}) copy-start(bf16[3,128,128]{2,1,0:T(8,128)(2,1)} %refs_4_.1) | copy-start | bytes 294916

commit v2 on v1

--- a/solution.py
+++ b/solution.py
@@ -41,9 +41,12 @@
 
 
 def kernel(plan, chunk_rows, tms, *refs):
-    x_ref, cot_ref, sw_ref, sb_ref, tw_ref, gin_ref, grads_ref, bias_ref = refs[:8]
-    next_cot, pad3, acc, res, cot_send, cot_recv = refs[8:14]
-    phases, position = [], 14
+    operands = refs[:5]
+    gin_ref, grads_ref, bias_ref = refs[5:8]
+    x_ref, cot_ref, sw_ref, sb_ref, tw_ref = held = refs[8:13]
+    held_sems = refs[13]
+    next_cot, pad3, acc, res, cot_send, cot_recv = refs[14:20]
+    phases, position = [], 20
     for _ in plan:
         phases.append(refs[position : position + 12])
         position += 12
@@ -76,11 +79,17 @@
         for m in range(1, 1 << len(group)):
             pl.semaphore_signal(barrier, inc=1, device_id=partner(group, m)[0], device_id_type=MESH)
             greeted += 1
+    x_in, cot_in, sw_in, sb_in, tw_in = fetch = [
+        pltpu.make_async_copy(operand, copy, held_sems.at[n])
+        for n, (operand, copy) in enumerate(zip(operands, held))
+    ]
+    for n in (0, 2, 3, 1, 4):
+        fetch[n].start()
     pl.semaphore_wait(barrier, greeted)
 
     tm = me["tm"]
     cot_copy = pltpu.make_async_remote_copy(
-        src_ref=cot_ref.at[0, pl.ds(0, 2)],
+        src_ref=operands[1].at[0, pl.ds(0, 2)],
         dst_ref=next_cot,
         send_sem=cot_send,
         recv_sem=cot_recv,
@@ -113,8 +122,11 @@
     pad3[:, pl.ds(0, width), :] = blank
     pad3[:, pl.ds(width + area, width), :] = blank
 
+    x_in.wait()
     x = x_ref[0].reshape(pixels, chan)
     fill(x.astype(F32), 1)
+    sw_in.wait()
+    sb_in.wait()
     pre = jnp.zeros((pixels, chan), F32)
     for i in range(3):
         pre = pre + jnp.dot(
@@ -127,6 +139,8 @@
     act_t = act.astype(F32).T.astype(BF16)
     x_t = x.astype(F32).T.astype(BF16)
 
+    cot_in.wait()
+    tw_in.wait()
     last = tm == tms - 1
 
     @pl.when(last)
@@ -316,13 +330,37 @@
         cot_copy.wait_send()
 
 
+def finish(cells, gin_ref, grads_ref, bias_ref, gin_out, sw_out, sb_out, tw_out, sw, sb, tw, sems):
+    norm = 1.0 / float(cells) ** 0.5
+    chan = gin_ref.shape[-1]
+    copies = [pltpu.make_async_copy(gin_ref, gin_out, sems.at[0])]
+    copies[0].start()
+    for k in range(3):
+        tw[k] = grads_ref[k * chan : (k + 1) * chan].astype(F32) * norm
+    copies.append(pltpu.make_async_copy(tw, tw_out, sems.at[1]))
+    copies[1].start()
+    sb[...] = jnp.sum(bias_ref[...], axis=0, keepdims=True) * norm
+    copies.append(pltpu.make_async_copy(sb, sb_out, sems.at[2]))
+    copies[2].start()
+    for i in range(3):
+        for j in range(3):
+            row = (3 + 3 * i + j) * chan
+            sw[i, j] = grads_ref[row : row + chan].astype(F32) * norm
+    copies.append(pltpu.make_async_copy(sw, sw_out, sems.at[3]))
+    copies[3].start()
+    for copy in copies:
+        copy.wait()
+
+
 def local(clips, tms, clip_in, cotangent, spatial_w, spatial_b, temporal_w):
     _, frames, height, width, chan = clip_in.shape
     assert frames == 2
     total_rows = 12 * chan
     chunk_rows = total_rows // CHUNKS
     plan = make_plan(clips, tms, chunk_rows)
-    scratch = [
+    operands = (clip_in, cotangent, spatial_w, spatial_b.reshape(1, chan), temporal_w)
+    scratch = [pltpu.VMEM(a.shape, a.dtype) for a in operands] + [
+        pltpu.SemaphoreType.DMA((5,)),
         pltpu.VMEM((2, height, width, chan), BF16),
         pltpu.VMEM((frames, (height + 2) * width, 3 * chan), BF16),
         pltpu.VMEM((CHUNKS, chunk_rows, chan), F32),
@@ -355,22 +393,27 @@
             jax.ShapeDtypeStruct((total_rows, chan), BF16),
             jax.ShapeDtypeStruct((8, chan), F32),
         ),
-        in_specs=[vmem] * 5,
+        in_specs=[pl.BlockSpec(memory_space=pltpu.HBM)] * 5,
         out_specs=(vmem, vmem, vmem),
         scratch_shapes=scratch,
         compiler_params=pltpu.CompilerParams(
             collective_id=0, has_side_effects=True, vmem_limit_bytes=48 * 1024 * 1024
         ),
         name="block_backward",
-    )(clip_in, cotangent, spatial_w, spatial_b.reshape(1, chan), temporal_w)
-    norm = 1.0 / jnp.sqrt(F32(clips * tms * frames * height * width))
-    grads = grads.astype(F32) * norm
-    return (
-        grad_in,
-        grads[3 * chan :].reshape(3, 3, chan, chan),
-        jnp.sum(bias, axis=0) * norm,
-        grads[: 3 * chan].reshape(3, chan, chan),
-    )
+    )(*[pltpu.with_memory_space_constraint(a, pltpu.HBM) for a in operands])
+    hbm = pl.BlockSpec(memory_space=pltpu.HBM)
+    shapes = [(clip_in.shape, BF16), (spatial_w.shape, F32), ((1, chan), F32), (temporal_w.shape, F32)]
+    cells = clips * tms * frames * height * width
+    grad_in, grad_sw, grad_sb, grad_tw = pl.pallas_call(
+        functools.partial(finish, cells),
+        out_shape=[jax.ShapeDtypeStruct(*s) for s in shapes],
+        in_specs=[vmem] * 3,
+        out_specs=[hbm] * 4,
+        scratch_shapes=[pltpu.VMEM(*s) for s in shapes[1:]] + [pltpu.SemaphoreType.DMA((4,))],
+        compiler_params=pltpu.CompilerParams(vmem_limit_bytes=24 * 1024 * 1024),
+        name="finish",
+    )(grad_in, grads, bias)
+    return grad_in, grad_sw, grad_sb.reshape(chan), grad_tw
 
 
 def solution(mesh):

time: 37.5 us -> 31.7 us (0.85)
  local copies, waits for them, and re-layouts: 6.51 us -> 0 us
  Pallas kernels: 29.6 us -> 30.9 us
  other arithmetic: 0.59 us -> 0 us
    unnamed x11 -> x0, local copies, waits for them, and re-layouts: 4.96 us -> none
    slice x2 -> x0, local copies, waits for them, and re-layouts: 1.54 us -> none  [the longest x1 0.85 us: local(): grads[3 * chan:].reshape(3, 3, chan, chan)]
    pallas_call x0 -> x1, Pallas kernels: none -> 0.96 us  [local(): pl.pallas_call(functools.partial(finish, cells), out_shape=[jax.ShapeDtyp...]
    mul x2 -> x0, other arithmetic: 0.57 us -> none  [the longest x1 0.52 us: local(): jnp.sum(bias, axis=0) * norm]
where the time goes in v2:
time: 31.7 us; the launch traced here: 31.5 us
  Pallas kernels  30.9 us (97%)
  between operations  0.64 us (2%)
    pallas_call x1, Pallas kernels, local(): pl.pallas_call(functools.partial(kernel, plan, chunk_rows, tms), out_shap...  29.9 us
    pallas_call x1, Pallas kernels, local(): pl.pallas_call(functools.partial(finish, cells), out_shape=[jax.ShapeDtyp...  0.96 us

profile of v2, /device:TPU:0, one launch (start us, length us, event | category | flops | bytes accessed | tf_op | source)
XLA Modules:
  0.0 31.5 jit_solution(8510394181497028286)
XLA Ops:
  0.6 29.9 %block_backward.1 = (bf16[1,2,8,32,128]{4,3,2,1,0:T(8,128)(2,1)S(1)}, bf16[1536,128]{1,0:T(8,128)(2,1)S(1)}, f32[8,128]{1,0:T(8,128)S(1)}) custom-call(bf16[1,2,8,32,128]{4,3,2,1,0:T(8,128)(2,1)} %refs_0_.1, bf16[1,2,8,32,128]{4,3,2,1,0:T(8,128)(2,1)} %refs_1_.1, bf16[3,3,128,128]{3,2,1,0:T(8,128)(2,1)} %refs_2_.1, f32[1,128]{1,0:T(1,128)} %bitcast.2, ...), custom_call_target="tpu_custom_call" | custom-call | tf_op jit(solution)/shard_map/block_backward/pallas_call | solution.py:389
  30.6 1.0 %finish.1 = (bf16[1,2,8,32,128]{4,3,2,1,0:T(8,128)(2,1)}, f32[3,3,128,128]{3,2,1,0:T(8,128)}, f32[1,128]{1,0:T(1,128)}, f32[3,128,128]{2,1,0:T(8,128)}) custom-call(bf16[1,2,8,32,128]{4,3,2,1,0:T(8,128)(2,1)S(1)} %get-tuple-element.11.gin_ref, bf16[1536,128]{1,0:T(8,128)(2,1)S(1)} %get-tuple-element.12.grads_ref, f32[8,128]{1,0:T(8,128)S(1)} %get-tuple-element.13.bias_ref), custom_call_target="tpu_custom_call" | custom-call | tf_op jit(solution)/shard_map/finish/pallas_call | solution.py:407

commit v3 on v2

--- a/solution.py
+++ b/solution.py
@@ -10,7 +10,7 @@
 MESH = pl.DeviceIdType.MESH
 F32, BF16 = jnp.float32, jnp.bfloat16
 TILE = 16
-CHUNKS = 1
+CHUNKS = 3
 
 
 def bits_of(size):
@@ -313,15 +313,18 @@
             grads_ref[pl.ds(c * chunk_rows, chunk_rows)] = res[c]
 
     phases[0][3][...] = jnp.sum(grad_pre32.reshape(pixels // 8, 8, chan), axis=0)
+    begun = 0
     for i in range(3):
         spatial_row(i)
-    for c in range(chunks):
-        advance(c, 0)
-    input_grad()
+        while begun < chunks and (begun + 1) * chunk_rows <= (6 + 3 * i) * chan:
+            advance(begun, 0)
+            begun += 1
     for step in range(1, len(steps) + chunks):
         for c in range(chunks):
             if 1 <= step - c <= len(steps):
                 advance(c, step - c)
+        if step == chunks:
+            input_grad()
     for copy in pending:
         copy.wait_send()
 

time: 31.7 us -> 36.8 us (1.16)
  Pallas kernels: 30.9 us -> 36 us
    pallas_call x1, Pallas kernels: 29.9 us -> 35 us  [local(): pl.pallas_call(functools.partial(kernel, plan, chunk_rows, tms), out_shap...]
where the time goes in v3:
time: 36.8 us; the launch traced here: 36.7 us
  Pallas kernels  36 us (98%)
  between operations  0.64 us (2%)
    pallas_call x1, Pallas kernels, local(): pl.pallas_call(functools.partial(kernel, plan, chunk_rows, tms), out_shap...  35 us
    pallas_call x1, Pallas kernels, local(): pl.pallas_call(functools.partial(finish, cells), out_shape=[jax.ShapeDtyp...  0.96 us

profile of v3, /device:TPU:0, one launch (start us, length us, event | category | flops | bytes accessed | tf_op | source)
XLA Modules:
  0.0 36.7 jit_solution(10078827791416576842)
XLA Ops:
  0.6 35.0 %block_backward.1 = (bf16[1,2,8,32,128]{4,3,2,1,0:T(8,128)(2,1)S(1)}, bf16[1536,128]{1,0:T(8,128)(2,1)S(1)}, f32[8,128]{1,0:T(8,128)S(1)}) custom-call(bf16[1,2,8,32,128]{4,3,2,1,0:T(8,128)(2,1)} %refs_0_.1, bf16[1,2,8,32,128]{4,3,2,1,0:T(8,128)(2,1)} %refs_1_.1, bf16[3,3,128,128]{3,2,1,0:T(8,128)(2,1)} %refs_2_.1, f32[1,128]{1,0:T(1,128)} %bitcast.2, ...), custom_call_target="tpu_custom_call" | custom-call | tf_op jit(solution)/shard_map/block_backward/pallas_call | solution.py:392
  35.7 1.0 %finish.1 = (bf16[1,2,8,32,128]{4,3,2,1,0:T(8,128)(2,1)}, f32[3,3,128,128]{3,2,1,0:T(8,128)}, f32[1,128]{1,0:T(1,128)}, f32[3,128,128]{2,1,0:T(8,128)}) custom-call(bf16[1,2,8,32,128]{4,3,2,1,0:T(8,128)(2,1)S(1)} %get-tuple-element.11.gin_ref, bf16[1536,128]{1,0:T(8,128)(2,1)S(1)} %get-tuple-element.12.grads_ref, f32[8,128]{1,0:T(8,128)S(1)} %get-tuple-element.13.bias_ref), custom_call_target="tpu_custom_call" | custom-call | tf_op jit(solution)/shard_map/finish/pallas_call | solution.py:410

commit v4 on v3

--- a/solution.py
+++ b/solution.py
@@ -10,7 +10,7 @@
 MESH = pl.DeviceIdType.MESH
 F32, BF16 = jnp.float32, jnp.bfloat16
 TILE = 16
-CHUNKS = 3
+CHUNKS = 1
 
 
 def bits_of(size):
@@ -19,15 +19,17 @@
     return count
 
 
+def make_groups(clips, tms):
+    clip_bits, tm_bits = bits_of(clips), bits_of(tms)
+    near = [("tm", b) for b in range(tm_bits)] + [("clip", b) for b in range(1, clip_bits) if b < 2]
+    far = [("clip", b) for b in range(2, clip_bits)]
+    return [("clip", 0)][:clip_bits], near, far
+
+
 def make_plan(clips, tms, rows):
-    clip_bits, tm_bits = bits_of(clips), bits_of(tms)
-    groups = [
-        [("clip", 0)][:clip_bits],
-        [("tm", b) for b in range(tm_bits)] + [("clip", b) for b in range(1, clip_bits) if b < 2],
-        [("clip", b) for b in range(2, clip_bits)],
-    ]
+    core, near, far = make_groups(clips, tms)
     plan = []
-    for order, group in enumerate(groups):
+    for order, group in enumerate([core, near + far]):
         kind = F32 if order == 0 else BF16
         cut = len(group)
         while rows % (TILE << cut):
@@ -40,7 +42,7 @@
     return plan
 
 
-def kernel(plan, chunk_rows, tms, *refs):
+def kernel(plan, bias_groups, chunk_rows, tms, *refs):
     operands = refs[:5]
     gin_ref, grads_ref, bias_ref = refs[5:8]
     x_ref, cot_ref, sw_ref, sb_ref, tw_ref = held = refs[8:13]
@@ -48,20 +50,25 @@
     next_cot, pad3, acc, res, cot_send, cot_recv = refs[14:20]
     phases, position = [], 20
     for _ in plan:
-        phases.append(refs[position : position + 12])
-        position += 12
+        phases.append(refs[position : position + 7])
+        position += 7
+    bias_parts = []
+    for _ in bias_groups:
+        bias_parts.append(refs[position : position + 4])
+        position += 4
     frames, height, width, chan = x_ref.shape[1:]
     area = height * width
     pixels = frames * area
     chunks = acc.shape[0]
     me = {"clip": lax.axis_index("clip"), "tm": lax.axis_index("tm")}
 
-    def bit(which):
-        axis, b = which
-        return lax.rem(me[axis] // (1 << b), 2)
+    bits = {}
+    for axis, size in (("clip", lax.axis_size("clip")), ("tm", tms)):
+        for b in range(bits_of(size)):
+            bits[axis, b] = lax.rem(me[axis] // (1 << b), 2)
 
     def group_index(group):
-        return sum((bit(w) * (1 << n) for n, w in enumerate(group)), 0)
+        return sum((bits[w] * (1 << n) for n, w in enumerate(group)), 0)
 
     def partner(group, m):
         to = dict(me)
@@ -69,23 +76,28 @@
         for n, which in enumerate(group):
             if (m >> n) & 1:
                 axis, b = which
-                to[axis] = to[axis] + (1 - 2 * bit(which)) * (1 << b)
-                index = index + (1 - 2 * bit(which)) * (1 << n)
+                step = 1 - 2 * bits[which]
+                to[axis] = to[axis] + step * (1 << b)
+                index = index + step * (1 << n)
         return to, index
 
     barrier = pltpu.get_barrier_semaphore()
-    greeted = 0
-    for group, *_ in plan:
+    greeted = set()
+    for group in [group for group, *_ in plan] + list(bias_groups):
         for m in range(1, 1 << len(group)):
-            pl.semaphore_signal(barrier, inc=1, device_id=partner(group, m)[0], device_id_type=MESH)
-            greeted += 1
+            key = frozenset(w for n, w in enumerate(group) if (m >> n) & 1)
+            if key not in greeted:
+                greeted.add(key)
+                pl.semaphore_signal(
+                    barrier, inc=1, device_id=partner(group, m)[0], device_id_type=MESH
+                )
     x_in, cot_in, sw_in, sb_in, tw_in = fetch = [
         pltpu.make_async_copy(operand, copy, held_sems.at[n])
         for n, (operand, copy) in enumerate(zip(operands, held))
     ]
     for n in (0, 2, 3, 1, 4):
         fetch[n].start()
-    pl.semaphore_wait(barrier, greeted)
+    pl.semaphore_wait(barrier, len(greeted))
 
     tm = me["tm"]
     cot_copy = pltpu.make_async_remote_copy(
@@ -203,8 +215,7 @@
 
     def reduce_start(c, p):
         group, scatter, rows, share, kind = plan[p]
-        cur, stage, recv, bsend, brecv = phases[p][:5]
-        ss, rs, bss, brs = phases[p][6:10]
+        cur, stage, recv, ss, rs = phases[p][:5]
         index = group_index(group)
         source = cur
         if p == 0:
@@ -215,7 +226,7 @@
         else:
             outgoing = source
         copies = []
-        for m in range(1, 1 << len(group)):
+        for m in reversed(range(1, 1 << len(group))):
             to, their = partner(group, m)
             src = outgoing.at[c, share_at(their, share)] if scatter else outgoing.at[c]
             copies.append(
@@ -230,43 +241,20 @@
                     )
                 )
             )
-            if c == chunks - 1:
-                copies.append(
-                    start(
-                        pltpu.make_async_remote_copy(
-                            src_ref=bsend,
-                            dst_ref=brecv.at[index],
-                            send_sem=bss.at[m],
-                            recv_sem=brs.at[m],
-                            device_id=to,
-                            device_id_type=MESH,
-                        )
-                    )
-                )
         waiting[c] = copies
 
     def reduce_end(c, p):
         group, scatter, rows, share, kind = plan[p]
-        cur, stage, recv, bsend, brecv = phases[p][:5]
+        cur, stage, recv = phases[p][:3]
         index = group_index(group)
         source = acc if p == 0 else cur
         own = source[c, share_at(index, share)] if scatter else source[c]
         recv[c, index] = own.astype(kind)
-        if c == chunks - 1:
-            brecv[index] = bsend[...]
         for copy in waiting[c]:
             copy.wait_recv()
         total = recv[c, 0].astype(F32)
         for n in range(1, 1 << len(group)):
             total = total + recv[c, n].astype(F32)
-        if c == chunks - 1:
-            bias = brecv[0]
-            for n in range(1, 1 << len(group)):
-                bias = bias + brecv[n]
-            if p + 1 < len(plan):
-                phases[p + 1][3][...] = bias
-            else:
-                bias_ref[...] = bias
         if p + 1 < len(plan):
             phases[p + 1][0][c] = total
         else:
@@ -274,10 +262,10 @@
 
     def gather_start(c, p):
         group, scatter, rows, share, kind = plan[p]
-        gs, gr = phases[p][10:12]
+        gs, gr = phases[p][5:7]
         copies = []
         mine = res.at[c, pl.ds(pl.multiple_of(offsets[p + 1], TILE), share)]
-        for m in range(1, 1 << len(group)):
+        for m in reversed(range(1, 1 << len(group))):
             to, _ = partner(group, m)
             copies.append(
                 start(
@@ -297,6 +285,42 @@
         for copy in waiting[c]:
             copy.wait_recv()
 
+    bias_waiting = []
+
+    def bias_start(q):
+        send, recv, bss, brs = bias_parts[q]
+        group = bias_groups[q]
+        index = group_index(group)
+        for m in range(1, 1 << len(group)):
+            bias_waiting.append(
+                start(
+                    pltpu.make_async_remote_copy(
+                        src_ref=send,
+                        dst_ref=recv.at[index],
+                        send_sem=bss.at[m],
+                        recv_sem=brs.at[m],
+                        device_id=partner(group, m)[0],
+                        device_id_type=MESH,
+                    )
+                )
+            )
+
+    def bias_end(q):
+        send, recv = bias_parts[q][:2]
+        recv[group_index(bias_groups[q])] = send[...]
+        while bias_waiting:
+            bias_waiting.pop().wait_recv()
+        total = recv[0]
+        for n in range(1, 1 << len(bias_groups[q])):
+            total = total + recv[n]
+        if q + 1 < len(bias_groups):
+            bias_parts[q + 1][0][...] = total
+            bias_start(q + 1)
+        else:
+            bias_ref[...] = total
+
+    bias_left = list(range(len(bias_groups)))
+
     steps = []
     for p in range(len(plan)):
         steps.append((reduce_start, reduce_end, p))
@@ -312,19 +336,24 @@
         else:
             grads_ref[pl.ds(c * chunk_rows, chunk_rows)] = res[c]
 
-    phases[0][3][...] = jnp.sum(grad_pre32.reshape(pixels // 8, 8, chan), axis=0)
+    bias_parts[0][0][...] = jnp.sum(grad_pre32.reshape(pixels // 8, 8, chan), axis=0)
     begun = 0
     for i in range(3):
         spatial_row(i)
         while begun < chunks and (begun + 1) * chunk_rows <= (6 + 3 * i) * chan:
             advance(begun, 0)
             begun += 1
+    bias_start(0)
     for step in range(1, len(steps) + chunks):
         for c in range(chunks):
             if 1 <= step - c <= len(steps):
                 advance(c, step - c)
         if step == chunks:
             input_grad()
+        for q in bias_left[:2]:
+            bias_end(bias_left.pop(0))
+    for q in bias_left:
+        bias_end(q)
     for copy in pending:
         copy.wait_send()
 
@@ -361,6 +390,7 @@
     total_rows = 12 * chan
     chunk_rows = total_rows // CHUNKS
     plan = make_plan(clips, tms, chunk_rows)
+    bias_groups = [tuple(g) for g in make_groups(clips, tms) if g]
     operands = (clip_in, cotangent, spatial_w, spatial_b.reshape(1, chan), temporal_w)
     scratch = [pltpu.VMEM(a.shape, a.dtype) for a in operands] + [
         pltpu.SemaphoreType.DMA((5,)),
@@ -378,19 +408,22 @@
             pltpu.VMEM((CHUNKS, rows, chan) if order else (1, 8, chan), F32),
             pltpu.VMEM((CHUNKS, rows, chan) if kind != F32 else (1, TILE, chan), BF16),
             pltpu.VMEM((CHUNKS, n, share, chan), kind),
-            pltpu.VMEM((8, chan), F32),
-            pltpu.VMEM((n, 8, chan), F32),
-            pltpu.VMEM((8, chan), F32),
             sems,
             sems,
-            pltpu.SemaphoreType.DMA((n,)),
-            pltpu.SemaphoreType.DMA((n,)),
             sems,
             sems,
         ]
+    for group in bias_groups:
+        n = 1 << len(group)
+        scratch += [
+            pltpu.VMEM((8, chan), F32),
+            pltpu.VMEM((n, 8, chan), F32),
+            pltpu.SemaphoreType.DMA((n,)),
+            pltpu.SemaphoreType.DMA((n,)),
+        ]
     vmem = pl.BlockSpec(memory_space=pltpu.VMEM)
     grad_in, grads, bias = pl.pallas_call(
-        functools.partial(kernel, plan, chunk_rows, tms),
+        functools.partial(kernel, plan, bias_groups, chunk_rows, tms),
         out_shape=(
             jax.ShapeDtypeStruct(clip_in.shape, BF16),
             jax.ShapeDtypeStruct((total_rows, chan), BF16),

time: 36.8 us -> 27.9 us (0.76)
  Pallas kernels: 36 us -> 27.1 us
    pallas_call x1, Pallas kernels: 35 us -> 26.2 us  [local(): pl.pallas_call(functools.partial(kernel, plan, bias_groups, chunk_rows, t...]
where the time goes in v4:
time: 27.9 us; the launch traced here: 27.8 us
  Pallas kernels  27.1 us (97%)
  between operations  0.64 us (2%)
    pallas_call x1, Pallas kernels, local(): pl.pallas_call(functools.partial(kernel, plan, bias_groups, chunk_rows, t...  26.2 us
    pallas_call x1, Pallas kernels, local(): pl.pallas_call(functools.partial(finish, cells), out_shape=[jax.ShapeDtyp...  0.96 us

profile of v4, /device:TPU:0, one launch (start us, length us, event | category | flops | bytes accessed | tf_op | source)
XLA Modules:
  0.0 27.8 jit_solution(6567103672842047074)
XLA Ops:
  0.6 26.2 %block_backward.1 = (bf16[1,2,8,32,128]{4,3,2,1,0:T(8,128)(2,1)S(1)}, bf16[1536,128]{1,0:T(8,128)(2,1)S(1)}, f32[8,128]{1,0:T(8,128)S(1)}) custom-call(bf16[1,2,8,32,128]{4,3,2,1,0:T(8,128)(2,1)} %refs_0_.1, bf16[1,2,8,32,128]{4,3,2,1,0:T(8,128)(2,1)} %refs_1_.1, bf16[3,3,128,128]{3,2,1,0:T(8,128)(2,1)} %refs_2_.1, f32[1,128]{1,0:T(1,128)} %bitcast.2, ...), custom_call_target="tpu_custom_call" | custom-call | tf_op jit(solution)/shard_map/block_backward/pallas_call | solution.py:425
  26.8 1.0 %finish.1 = (bf16[1,2,8,32,128]{4,3,2,1,0:T(8,128)(2,1)}, f32[3,3,128,128]{3,2,1,0:T(8,128)}, f32[1,128]{1,0:T(1,128)}, f32[3,128,128]{2,1,0:T(8,128)}) custom-call(bf16[1,2,8,32,128]{4,3,2,1,0:T(8,128)(2,1)S(1)} %get-tuple-element.11.gin_ref, bf16[1536,128]{1,0:T(8,128)(2,1)S(1)} %get-tuple-element.12.grads_ref, f32[8,128]{1,0:T(8,128)S(1)} %get-tuple-element.13.bias_ref), custom_call_target="tpu_custom_call" | custom-call | tf_op jit(solution)/shard_map/finish/pallas_call | solution.py:443

commit v5 on v4

--- a/solution.py
+++ b/solution.py
@@ -29,8 +29,8 @@
 def make_plan(clips, tms, rows):
     core, near, far = make_groups(clips, tms)
     plan = []
-    for order, group in enumerate([core, near + far]):
-        kind = F32 if order == 0 else BF16
+    for group in [core, near + far]:
+        kind = BF16
         cut = len(group)
         while rows % (TILE << cut):
             cut -= 1
@@ -58,7 +58,6 @@
         position += 4
     frames, height, width, chan = x_ref.shape[1:]
     area = height * width
-    pixels = frames * area
     chunks = acc.shape[0]
     me = {"clip": lax.axis_index("clip"), "tm": lax.axis_index("tm")}
 
@@ -100,103 +99,111 @@
     pl.semaphore_wait(barrier, len(greeted))
 
     tm = me["tm"]
-    cot_copy = pltpu.make_async_remote_copy(
-        src_ref=operands[1].at[0, pl.ds(0, 2)],
-        dst_ref=next_cot,
-        send_sem=cot_send,
-        recv_sem=cot_recv,
-        device_id={"clip": me["clip"], "tm": jnp.maximum(tm - 1, 0)},
-        device_id_type=MESH,
-    )
+    cot_copies = [
+        pltpu.make_async_remote_copy(
+            src_ref=operands[1].at[0, u],
+            dst_ref=next_cot.at[u],
+            send_sem=cot_send.at[u],
+            recv_sem=cot_recv.at[u],
+            device_id={"clip": me["clip"], "tm": jnp.maximum(tm - 1, 0)},
+            device_id_type=MESH,
+        )
+        for u in range(frames)
+    ]
+    last = tm == tms - 1
 
     @pl.when(tm > 0)
     def _():
-        cot_copy.start()
-
-    column = lax.broadcasted_iota(jnp.int32, (pixels, chan), 0) % width
+        for copy in cot_copies:
+            copy.start()
+
+    @pl.when(last)
+    def _():
+        next_cot[...] = jnp.zeros_like(next_cot)
+
+    column = lax.broadcasted_iota(jnp.int32, (area, chan), 0) % width
 
     def column_shift(flat, d):
         if d == 0:
             return flat.astype(BF16)
-        rolled = pltpu.roll(flat, (-d) % pixels, 0)
+        rolled = pltpu.roll(flat, (-d) % area, 0)
         edge = width - 1 if d == 1 else 0
         return jnp.where(column == edge, 0.0, rolled).astype(BF16)
 
-    def fill(flat, sign):
+    def fill(u, flat, sign):
         for j in range(3):
-            moved = column_shift(flat, sign * (j - 1)).reshape(frames, area, chan)
-            pad3[:, pl.ds(width, area), pl.ds(j * chan, chan)] = moved
-
-    def window(start):
-        return pad3[:, pl.ds(start * width, area), :].reshape(pixels, 3 * chan)
-
+            moved = column_shift(flat, sign * (j - 1))
+            pad3[u, pl.ds(width, area), pl.ds(j * chan, chan)] = moved
+
+    def window(u, start):
+        return pad3[u, pl.ds(start * width, area), :]
+
+    x_in.wait()
     blank = jnp.zeros((frames, width, 3 * chan), BF16)
     pad3[:, pl.ds(0, width), :] = blank
     pad3[:, pl.ds(width + area, width), :] = blank
 
-    x_in.wait()
-    x = x_ref[0].reshape(pixels, chan)
-    fill(x.astype(F32), 1)
-    sw_in.wait()
-    sb_in.wait()
-    pre = jnp.zeros((pixels, chan), F32)
-    for i in range(3):
-        pre = pre + jnp.dot(
-            window(i), sw_ref[i].reshape(3 * chan, chan), preferred_element_type=F32
-        )
-    pre = pre + sb_ref[...]
-    sig = 1.0 / (1.0 + jnp.exp(-pre))
-    act = (pre * sig).astype(BF16)
-    slope = sig * (1.0 + pre * (1.0 - sig))
-    act_t = act.astype(F32).T.astype(BF16)
-    x_t = x.astype(F32).T.astype(BF16)
+    frame_data = []
+    for u in range(frames):
+        x = x_ref[0, u].reshape(area, chan).astype(F32)
+        fill(u, x, 1)
+        if u == 0:
+            sw_in.wait()
+            sb_in.wait()
+        pre = jnp.zeros((area, chan), F32)
+        for i in range(3):
+            pre = pre + jnp.dot(
+                window(u, i), sw_ref[i].reshape(3 * chan, chan), preferred_element_type=F32
+            )
+        pre = pre + sb_ref[...]
+        sig = 1.0 / (1.0 + jnp.exp(-pre))
+        act = (pre * sig).astype(BF16)
+        slope = sig * (1.0 + pre * (1.0 - sig))
+        frame_data.append((x.T.astype(BF16), act.astype(F32).T.astype(BF16), slope))
 
     cot_in.wait()
     tw_in.wait()
-    last = tm == tms - 1
-
-    @pl.when(last)
-    def _():
-        next_cot[...] = jnp.zeros_like(next_cot)
-
-    @pl.when(jnp.logical_not(last))
-    def _():
-        cot_copy.wait_recv()
-
-    cot = cot_ref[0].reshape(pixels, chan)
-    after = next_cot[...].reshape(2 * area, chan)
-    later = [cot]
-    for k in (1, 2):
-        kept = [cot[k * area :]] if k < frames else []
-        later.append(jnp.concatenate(kept + [after[: k * area]], axis=0))
-    later = jnp.concatenate(later, axis=1)
     nt = (((1,), (1,)), ((), ()))
     tw = jnp.concatenate([tw_ref[k] for k in range(3)], axis=1)
-    grad_act = lax.dot_general(later, tw, nt, preferred_element_type=F32).astype(BF16)
-    grad_pre = (grad_act.astype(F32) * slope).astype(BF16)
-    grad_pre32 = grad_pre.astype(F32)
-    fill(grad_pre32, -1)
-
-    def put(block, value):
+
+    def cot_frame(v):
+        source = cot_ref[0, v] if v < frames else next_cot[v - frames]
+        return source.reshape(area, chan)
+
+    def put(u, block, value):
         row = block * chan
         c = row // chunk_rows
-        acc[c, pl.ds(row - c * chunk_rows, chan), :] = value
-
-    grad_tw = jnp.dot(act_t, later, preferred_element_type=F32)
-    for k in range(3):
-        put(k, grad_tw[:, k * chan : (k + 1) * chan])
-
-    def spatial_row(i):
-        grad = jnp.dot(x_t, window(2 - i), preferred_element_type=F32)
-        for j in range(3):
-            put(3 + 3 * i + j, grad[:, j * chan : (j + 1) * chan])
-
-    def input_grad():
-        total = cot.astype(F32)
+        at = (c, pl.ds(row - c * chunk_rows, chan), slice(None))
+        acc[at] = value if u == 0 else acc[at] + value
+
+    def frame_back(u):
+        x_t, act_t, slope = frame_data[u]
+
+        @pl.when(jnp.logical_not(last))
+        def _():
+            cot_copies[u].wait_recv()
+
+        later = jnp.concatenate([cot_frame(u + k) for k in range(3)], axis=1)
+        grad_act = lax.dot_general(later, tw, nt, preferred_element_type=F32).astype(BF16)
+        grad_pre = (grad_act.astype(F32) * slope).astype(BF16).astype(F32)
+        fill(u, grad_pre, -1)
+        grad_tw = jnp.dot(act_t, later, preferred_element_type=F32)
+        for k in range(3):
+            put(u, k, grad_tw[:, k * chan : (k + 1) * chan])
+        for i in range(3):
+            grad = jnp.dot(x_t, window(u, 2 - i), preferred_element_type=F32)
+            for j in range(3):
+                put(u, 3 + 3 * i + j, grad[:, j * chan : (j + 1) * chan])
+        bias = jnp.sum(grad_pre.reshape(area // 8, 8, chan), axis=0)
+        part = bias_parts[0][0]
+        part[...] = bias if u == 0 else part[...] + bias
+
+    def input_grad(u):
+        total = cot_frame(u).astype(F32)
         for i in range(3):
             sw = jnp.concatenate([sw_ref[i, j] for j in range(3)], axis=1)
-            total = total + lax.dot_general(window(2 - i), sw, nt, preferred_element_type=F32)
-        gin_ref[0] = total.astype(BF16).reshape(frames, height, width, chan)
+            total = total + lax.dot_general(window(u, 2 - i), sw, nt, preferred_element_type=F32)
+        gin_ref[0, u] = total.astype(BF16).reshape(height, width, chan)
 
     offsets = [0]
     for group, scatter, _, share, _ in plan:
@@ -221,7 +228,11 @@
         if p == 0:
             source = acc
         if kind != F32:
-            stage[c] = source[c].astype(kind)
+            if scatter and len(group) == 1:
+                theirs = share_at(partner(group, 1)[1], share)
+                stage[c, theirs] = source[c, theirs].astype(kind)
+            else:
+                stage[c] = source[c].astype(kind)
             outgoing = stage
         else:
             outgoing = source
@@ -249,9 +260,9 @@
         index = group_index(group)
         source = acc if p == 0 else cur
         own = source[c, share_at(index, share)] if scatter else source[c]
-        recv[c, index] = own.astype(kind)
         for copy in waiting[c]:
             copy.wait_recv()
+        recv[c, index] = own.astype(kind)
         total = recv[c, 0].astype(F32)
         for n in range(1, 1 << len(group)):
             total = total + recv[c, n].astype(F32)
@@ -336,20 +347,19 @@
         else:
             grads_ref[pl.ds(c * chunk_rows, chunk_rows)] = res[c]
 
-    bias_parts[0][0][...] = jnp.sum(grad_pre32.reshape(pixels // 8, 8, chan), axis=0)
-    begun = 0
-    for i in range(3):
-        spatial_row(i)
-        while begun < chunks and (begun + 1) * chunk_rows <= (6 + 3 * i) * chan:
-            advance(begun, 0)
-            begun += 1
+    for u in range(frames):
+        frame_back(u)
+        if u + 1 < frames:
+            input_grad(u)
+    for c in range(chunks):
+        advance(c, 0)
     bias_start(0)
     for step in range(1, len(steps) + chunks):
         for c in range(chunks):
             if 1 <= step - c <= len(steps):
                 advance(c, step - c)
         if step == chunks:
-            input_grad()
+            input_grad(frames - 1)
         for q in bias_left[:2]:
             bias_end(bias_left.pop(0))
     for q in bias_left:
@@ -359,7 +369,8 @@
 
     @pl.when(tm > 0)
     def _():
-        cot_copy.wait_send()
+        for copy in cot_copies:
+            copy.wait_send()
 
 
 def finish(cells, gin_ref, grads_ref, bias_ref, gin_out, sw_out, sb_out, tw_out, sw, sb, tw, sems):
@@ -398,8 +409,8 @@
         pltpu.VMEM((frames, (height + 2) * width, 3 * chan), BF16),
         pltpu.VMEM((CHUNKS, chunk_rows, chan), F32),
         pltpu.VMEM((CHUNKS, chunk_rows, chan), BF16),
-        pltpu.SemaphoreType.DMA,
-        pltpu.SemaphoreType.DMA,
+        pltpu.SemaphoreType.DMA((2,)),
+        pltpu.SemaphoreType.DMA((2,)),
     ]
     for order, (group, scatter, rows, share, kind) in enumerate(plan):
         n = 1 << len(group)

time: 27.9 us -> 27.7 us (level)
  no operation moved by 1% of the time
where the time goes in v5:
time: 27.7 us; the launch traced here: 27.5 us
  Pallas kernels  26.9 us (97%)
  between operations  0.64 us (2%)
    pallas_call x1, Pallas kernels, local(): pl.pallas_call(functools.partial(kernel, plan, bias_groups, chunk_rows, t...  25.9 us
    pallas_call x1, Pallas kernels, local(): pl.pallas_call(functools.partial(finish, cells), out_shape=[jax.ShapeDtyp...  0.96 us

profile of v5, /device:TPU:0, one launch (start us, length us, event | category | flops | bytes accessed | tf_op | source)
XLA Modules:
  0.0 27.5 jit_solution(15029757010106736462)
XLA Ops:
  0.6 25.9 %block_backward.1 = (bf16[1,2,8,32,128]{4,3,2,1,0:T(8,128)(2,1)S(1)}, bf16[1536,128]{1,0:T(8,128)(2,1)S(1)}, f32[8,128]{1,0:T(8,128)S(1)}) custom-call(bf16[1,2,8,32,128]{4,3,2,1,0:T(8,128)(2,1)} %refs_0_.1, bf16[1,2,8,32,128]{4,3,2,1,0:T(8,128)(2,1)} %refs_1_.1, bf16[3,3,128,128]{3,2,1,0:T(8,128)(2,1)} %refs_2_.1, f32[1,128]{1,0:T(1,128)} %bitcast.2, ...), custom_call_target="tpu_custom_call" | custom-call | tf_op jit(solution)/shard_map/block_backward/pallas_call | solution.py:436
  26.6 1.0 %finish.1 = (bf16[1,2,8,32,128]{4,3,2,1,0:T(8,128)(2,1)}, f32[3,3,128,128]{3,2,1,0:T(8,128)}, f32[1,128]{1,0:T(1,128)}, f32[3,128,128]{2,1,0:T(8,128)}) custom-call(bf16[1,2,8,32,128]{4,3,2,1,0:T(8,128)(2,1)S(1)} %get-tuple-element.11.gin_ref, bf16[1536,128]{1,0:T(8,128)(2,1)S(1)} %get-tuple-element.12.grads_ref, f32[8,128]{1,0:T(8,128)S(1)} %get-tuple-element.13.bias_ref), custom_call_target="tpu_custom_call" | custom-call | tf_op jit(solution)/shard_map/finish/pallas_call | solution.py:454

commit v6 on v5

--- a/solution.py
+++ b/solution.py
@@ -237,6 +237,26 @@
         else:
             outgoing = source
         copies = []
+        if scatter and len(group) > 1:
+            half = 1 << (len(group) - 1)
+            low = group_index(group[:-1])
+            for other in (half, 0):
+                for m in range(1, half):
+                    share_of = share_at(partner(group, m + other)[1], share)
+                    copies.append(
+                        start(
+                            pltpu.make_async_remote_copy(
+                                src_ref=outgoing.at[c, share_of],
+                                dst_ref=recv.at[c, other + low],
+                                send_sem=ss.at[c, m + other],
+                                recv_sem=rs.at[c, m + other],
+                                device_id=partner(group, m)[0],
+                                device_id_type=MESH,
+                            )
+                        )
+                    )
+            waiting[c] = copies
+            return
         for m in reversed(range(1, 1 << len(group))):
             to, their = partner(group, m)
             src = outgoing.at[c, share_at(their, share)] if scatter else outgoing.at[c]
@@ -260,36 +280,85 @@
         index = group_index(group)
         source = acc if p == 0 else cur
         own = source[c, share_at(index, share)] if scatter else source[c]
-        for copy in waiting[c]:
-            copy.wait_recv()
-        recv[c, index] = own.astype(kind)
-        total = recv[c, 0].astype(F32)
-        for n in range(1, 1 << len(group)):
-            total = total + recv[c, n].astype(F32)
+        if scatter and len(group) > 1:
+            total = halves_end(c, p, own)
+        else:
+            total = plain_end(c, p, own)
         if p + 1 < len(plan):
             phases[p + 1][0][c] = total
         else:
             res[c, pl.ds(pl.multiple_of(offsets[-1], TILE), share)] = total.astype(BF16)
 
+    def plain_end(c, p, own):
+        group, kind, recv = plan[p][0], plan[p][4], phases[p][2]
+        recv[c, group_index(group)] = own.astype(kind)
+        for copy in waiting[c]:
+            copy.wait_recv()
+        total = recv[c, 0].astype(F32)
+        for n in range(1, 1 << len(group)):
+            total = total + recv[c, n].astype(F32)
+        return total
+
+    def halves_end(c, p, own):
+        group, _, _, share, kind = plan[p]
+        cur, _, recv, ss, rs = phases[p][:5]
+        source = acc if p == 0 else cur
+        count = 1 << len(group)
+        half = count // 2
+        low = group_index(group[:-1])
+        to, across = partner(group, half)
+        recv[c, half + low] = source[c, share_at(across, share)].astype(kind)
+        for copy in waiting[c][: half - 1]:
+            copy.wait_recv()
+        total = recv[c, half].astype(F32)
+        for n in range(half + 1, count):
+            total = total + recv[c, n].astype(F32)
+        recv[c, count] = total.astype(kind)
+        cross = start(
+            pltpu.make_async_remote_copy(
+                src_ref=recv.at[c, count],
+                dst_ref=recv.at[c, count + 1],
+                send_sem=ss.at[c, half],
+                recv_sem=rs.at[c, half],
+                device_id=to,
+                device_id_type=MESH,
+            )
+        )
+        recv[c, low] = own.astype(kind)
+        for copy in waiting[c][half - 1 :]:
+            copy.wait_recv()
+        total = recv[c, 0].astype(F32)
+        for n in range(1, half):
+            total = total + recv[c, n].astype(F32)
+        cross.wait_recv()
+        return total + recv[c, count + 1].astype(F32)
+
     def gather_start(c, p):
         group, scatter, rows, share, kind = plan[p]
         gs, gr = phases[p][5:7]
-        copies = []
-        mine = res.at[c, pl.ds(pl.multiple_of(offsets[p + 1], TILE), share)]
-        for m in reversed(range(1, 1 << len(group))):
-            to, _ = partner(group, m)
-            copies.append(
-                start(
-                    pltpu.make_async_remote_copy(
-                        src_ref=mine,
-                        dst_ref=mine,
-                        send_sem=gs.at[c, m],
-                        recv_sem=gr.at[c, m],
-                        device_id=to,
-                        device_id_type=MESH,
-                    )
+        def piece(index):
+            row = pl.multiple_of(offsets[p] + index * share, TILE)
+            return res.at[c, pl.ds(row, share)]
+
+        def send(index, m, sem):
+            return start(
+                pltpu.make_async_remote_copy(
+                    src_ref=piece(index),
+                    dst_ref=piece(index),
+                    send_sem=gs.at[c, sem],
+                    recv_sem=gr.at[c, sem],
+                    device_id=partner(group, m)[0],
+                    device_id_type=MESH,
                 )
             )
+
+        half = 1 << (len(group) - 1)
+        index = group_index(group)
+        cross = send(index, half, half)
+        copies = [send(index, m, m) for m in range(1, half)]
+        cross.wait_recv()
+        across = partner(group, half)[1]
+        copies += [send(across, m, m + half) for m in range(1, half)]
         waiting[c] = copies
 
     def gather_end(c, p):
@@ -360,7 +429,7 @@
                 advance(c, step - c)
         if step == chunks:
             input_grad(frames - 1)
-        for q in bias_left[:2]:
+        for q in bias_left[:1]:
             bias_end(bias_left.pop(0))
     for q in bias_left:
         bias_end(q)
@@ -418,7 +487,7 @@
         scratch += [
             pltpu.VMEM((CHUNKS, rows, chan) if order else (1, 8, chan), F32),
             pltpu.VMEM((CHUNKS, rows, chan) if kind != F32 else (1, TILE, chan), BF16),
-            pltpu.VMEM((CHUNKS, n, share, chan), kind),
+            pltpu.VMEM((CHUNKS, n + 2, share, chan), kind),
             sems,
             sems,
             sems,

time: 27.7 us -> 30.1 us (1.087)
  Pallas kernels: 26.9 us -> 29.3 us
    pallas_call x1, Pallas kernels: 25.9 us -> 28.3 us  [local(): pl.pallas_call(functools.partial(kernel, plan, bias_groups, chunk_rows, t...]
where the time goes in v6:
time: 30.1 us; the launch traced here: 29.9 us
  Pallas kernels  29.3 us (97%)
  between operations  0.64 us (2%)
    pallas_call x1, Pallas kernels, local(): pl.pallas_call(functools.partial(kernel, plan, bias_groups, chunk_rows, t...  28.3 us
    pallas_call x1, Pallas kernels, local(): pl.pallas_call(functools.partial(finish, cells), out_shape=[jax.ShapeDtyp...  0.96 us

profile of v6, /device:TPU:0, one launch (start us, length us, event | category | flops | bytes accessed | tf_op | source)
XLA Modules:
  0.0 29.9 jit_solution(2556169772627523471)
XLA Ops:
  0.6 28.3 %block_backward.1 = (bf16[1,2,8,32,128]{4,3,2,1,0:T(8,128)(2,1)S(1)}, bf16[1536,128]{1,0:T(8,128)(2,1)S(1)}, f32[8,128]{1,0:T(8,128)S(1)}) custom-call(bf16[1,2,8,32,128]{4,3,2,1,0:T(8,128)(2,1)} %refs_0_.1, bf16[1,2,8,32,128]{4,3,2,1,0:T(8,128)(2,1)} %refs_1_.1, bf16[3,3,128,128]{3,2,1,0:T(8,128)(2,1)} %refs_2_.1, f32[1,128]{1,0:T(1,128)} %bitcast.2, ...), custom_call_target="tpu_custom_call" | custom-call | tf_op jit(solution)/shard_map/block_backward/pallas_call | solution.py:505
  29.0 1.0 %finish.1 = (bf16[1,2,8,32,128]{4,3,2,1,0:T(8,128)(2,1)}, f32[3,3,128,128]{3,2,1,0:T(8,128)}, f32[1,128]{1,0:T(1,128)}, f32[3,128,128]{2,1,0:T(8,128)}) custom-call(bf16[1,2,8,32,128]{4,3,2,1,0:T(8,128)(2,1)S(1)} %get-tuple-element.11.gin_ref, bf16[1536,128]{1,0:T(8,128)(2,1)S(1)} %get-tuple-element.12.grads_ref, f32[8,128]{1,0:T(8,128)S(1)} %get-tuple-element.13.bias_ref), custom_call_target="tpu_custom_call" | custom-call | tf_op jit(solution)/shard_map/finish/pallas_call | solution.py:523

commit v7 on v5

--- a/solution.py
+++ b/solution.py
@@ -50,12 +50,13 @@
     next_cot, pad3, acc, res, cot_send, cot_recv = refs[14:20]
     phases, position = [], 20
     for _ in plan:
-        phases.append(refs[position : position + 7])
-        position += 7
+        phases.append(refs[position : position + 5])
+        position += 5
     bias_parts = []
     for _ in bias_groups:
         bias_parts.append(refs[position : position + 4])
         position += 4
+    gather_sems = refs[position:]
     frames, height, width, chan = x_ref.shape[1:]
     area = height * width
     chunks = acc.shape[0]
@@ -82,7 +83,8 @@
 
     barrier = pltpu.get_barrier_semaphore()
     greeted = set()
-    for group in [group for group, *_ in plan] + list(bias_groups):
+    everyone = tuple(w for group, scatter, *_ in plan if scatter for w in group)
+    for group in [group for group, *_ in plan] + list(bias_groups) + [everyone]:
         for m in range(1, 1 << len(group)):
             key = frozenset(w for n, w in enumerate(group) if (m >> n) & 1)
             if key not in greeted:
@@ -272,12 +274,11 @@
             res[c, pl.ds(pl.multiple_of(offsets[-1], TILE), share)] = total.astype(BF16)
 
     def gather_start(c, p):
-        group, scatter, rows, share, kind = plan[p]
-        gs, gr = phases[p][5:7]
+        gs, gr = gather_sems
+        share = plan[-1][3]
+        mine = res.at[c, pl.ds(pl.multiple_of(offsets[-1], TILE), share)]
         copies = []
-        mine = res.at[c, pl.ds(pl.multiple_of(offsets[p + 1], TILE), share)]
-        for m in reversed(range(1, 1 << len(group))):
-            to, _ = partner(group, m)
+        for m in reversed(range(1, 1 << len(everyone))):
             copies.append(
                 start(
                     pltpu.make_async_remote_copy(
@@ -285,7 +286,7 @@
                         dst_ref=mine,
                         send_sem=gs.at[c, m],
                         recv_sem=gr.at[c, m],
-                        device_id=to,
+                        device_id=partner(everyone, m)[0],
                         device_id_type=MESH,
                     )
                 )
@@ -335,9 +336,8 @@
     steps = []
     for p in range(len(plan)):
         steps.append((reduce_start, reduce_end, p))
-    for p in reversed(range(len(plan))):
-        if plan[p][1]:
-            steps.append((gather_start, gather_end, p))
+    if everyone:
+        steps.append((gather_start, gather_end, 0))
 
     def advance(c, k):
         if k > 0:
@@ -421,8 +421,6 @@
             pltpu.VMEM((CHUNKS, n, share, chan), kind),
             sems,
             sems,
-            sems,
-            sems,
         ]
     for group in bias_groups:
         n = 1 << len(group)
@@ -432,6 +430,8 @@
             pltpu.SemaphoreType.DMA((n,)),
             pltpu.SemaphoreType.DMA((n,)),
         ]
+    reached = 1 << sum(len(group) for group, scatter, *_ in plan if scatter)
+    scratch += [pltpu.SemaphoreType.DMA((CHUNKS, reached))] * 2
     vmem = pl.BlockSpec(memory_space=pltpu.VMEM)
     grad_in, grads, bias = pl.pallas_call(
         functools.partial(kernel, plan, bias_groups, chunk_rows, tms),

time: 27.7 us -> 32.4 us (1.17)
  Pallas kernels: 26.9 us -> 31.6 us
    pallas_call x1, Pallas kernels: 25.9 us -> 30.7 us  [local(): pl.pallas_call(functools.partial(kernel, plan, bias_groups, chunk_rows, t...]
where the time goes in v7:
time: 32.4 us; the launch traced here: 32.3 us
  Pallas kernels  31.6 us (98%)
  between operations  0.64 us (2%)
    pallas_call x1, Pallas kernels, local(): pl.pallas_call(functools.partial(kernel, plan, bias_groups, chunk_rows, t...  30.7 us
    pallas_call x1, Pallas kernels, local(): pl.pallas_call(functools.partial(finish, cells), out_shape=[jax.ShapeDtyp...  0.96 us

profile of v7, /device:TPU:0, one launch (start us, length us, event | category | flops | bytes accessed | tf_op | source)
XLA Modules:
  0.0 32.3 jit_solution(15194268628094600651)
XLA Ops:
  0.6 30.7 %block_backward.1 = (bf16[1,2,8,32,128]{4,3,2,1,0:T(8,128)(2,1)S(1)}, bf16[1536,128]{1,0:T(8,128)(2,1)S(1)}, f32[8,128]{1,0:T(8,128)S(1)}) custom-call(bf16[1,2,8,32,128]{4,3,2,1,0:T(8,128)(2,1)} %refs_0_.1, bf16[1,2,8,32,128]{4,3,2,1,0:T(8,128)(2,1)} %refs_1_.1, bf16[3,3,128,128]{3,2,1,0:T(8,128)(2,1)} %refs_2_.1, f32[1,128]{1,0:T(1,128)} %bitcast.2, ...), custom_call_target="tpu_custom_call" | custom-call | tf_op jit(solution)/shard_map/block_backward/pallas_call | solution.py:436
  31.3 1.0 %finish.1 = (bf16[1,2,8,32,128]{4,3,2,1,0:T(8,128)(2,1)}, f32[3,3,128,128]{3,2,1,0:T(8,128)}, f32[1,128]{1,0:T(1,128)}, f32[3,128,128]{2,1,0:T(8,128)}) custom-call(bf16[1,2,8,32,128]{4,3,2,1,0:T(8,128)(2,1)S(1)} %get-tuple-element.11.gin_ref, bf16[1536,128]{1,0:T(8,128)(2,1)S(1)} %get-tuple-element.12.grads_ref, f32[8,128]{1,0:T(8,128)S(1)} %get-tuple-element.13.bias_ref), custom_call_target="tpu_custom_call" | custom-call | tf_op jit(solution)/shard_map/finish/pallas_call | solution.py:454
